TPU v7x, 128 devices: a whole 4x4x4 slice. The times are simulated.
128 devices in a mesh: qx: 16 (over z, x), qy: 8 (over y, core).
Axes of the slice: x: 4, y: 4, z: 4, core: 2. Of those that a mesh axis runs over, the one named last changes fastest.
Arguments:
- dynamical: float32 [2, 64, 64, 9216], P(None, 'qx', 'qy'), may hold values from -0.15 to 1.5, as said below
Outputs:
- green_space: float32 [2, 64, 64, 9216], P(None, 'qx', 'qy')
Inputs may be any that keep to these rules, and one draw needn't show every extreme that they name: `dynamical`: every q-point's matrix is Hermitian: the real part symmetric, the imaginary part antisymmetric with a zero diagonal; the real diagonal lies in 0.75 to 1.5.
All inputs are finite; a program needn't handle non-finite values.
Results may differ from a plain program's by a relative error of at most 0.00023.
Values sent between devices are 32-bit elements; how exact they have to be, the bound alone decides.
A program may use at most 64 MiB of HBM per device.

v0:
```python
import math

import jax
import jax.numpy as jnp
from jax import lax
from jax.sharding import PartitionSpec as P

M = 96
ITERS = 3


shift_eta = 0.25


def cmatmul(ar, ai, br, bi):
    hp = lax.Precision.HIGHEST
    real_part = jnp.matmul(ar, br, precision=hp) - jnp.matmul(ai, bi, precision=hp)
    imag_part = jnp.matmul(ar, bi, precision=hp) + jnp.matmul(ai, br, precision=hp)
    return (real_part, imag_part)


def newton_schulz(real_in, imag_in, size, steps):
    identity = jnp.eye(size, dtype=jnp.float32)
    diag_vals = jnp.diagonal(real_in, axis1=1, axis2=2)
    denom = diag_vals * diag_vals + shift_eta * shift_eta
    xr = identity[None] * (diag_vals / denom)[:, None, :]
    xi = identity[None] * (-shift_eta / denom)[:, None, :]
    ai = imag_in + shift_eta * identity[None]
    for step in range(steps):
        yr, yi = cmatmul(real_in, ai, xr, xi)
        zr = 2.0 * identity[None] - yr
        zi = -yi
        xr, xi = cmatmul(xr, xi, zr, zi)
    return (xr, xi)


def tables(length):
    index = jnp.arange(length, dtype=jnp.int32)
    product = index[:, None] * index[None, :] % length
    angle = product.astype(jnp.float32) * (2.0 * math.pi / length)
    scale = 1.0 / math.sqrt(length)
    return (jnp.cos(angle) * scale, jnp.sin(angle) * scale)


def combine(cosine, sine, real, imag, form):
    hp = lax.Precision.HIGHEST
    out_r = jnp.einsum(form, cosine, real, precision=hp) - jnp.einsum(
        form, sine, imag, precision=hp
    )
    out_i = jnp.einsum(form, sine, real, precision=hp) + jnp.einsum(
        form, cosine, imag, precision=hp
    )
    return (out_r, out_i)


def per_device(dynamical):
    local_x = dynamical.shape[1]
    local_y = dynamical.shape[2]
    entries = dynamical.shape[3]
    count = local_x * local_y
    real_in = dynamical[0].reshape(count, M, M)
    imag_in = dynamical[1].reshape(count, M, M)
    xr, xi = newton_schulz(real_in, imag_in, M, ITERS)
    size_x = lax.axis_size("qx")
    size_y = lax.axis_size("qy")
    full_x = local_x * size_x
    full_y = local_y * size_y
    cos_x, sin_x = tables(full_x)
    cos_y, sin_y = tables(full_y)
    width_x = entries // size_x
    part_r = xr.reshape(local_x, local_y, size_x, width_x)
    part_i = xi.reshape(local_x, local_y, size_x, width_x)
    pieces = (
        lax.all_to_all(part_r, "qx", split_axis=2, concat_axis=0, tiled=True),
        lax.all_to_all(part_i, "qx", split_axis=2, concat_axis=0, tiled=True),
    )
    first_r, first_i = combine(cos_x, sin_x, pieces[0], pieces[1], "rq,qiak->riak")
    back_r, back_i = (
        lax.all_to_all(first_r, "qx", split_axis=0, concat_axis=2, tiled=True),
        lax.all_to_all(first_i, "qx", split_axis=0, concat_axis=2, tiled=True),
    )
    width_y = entries // size_y
    back_r = back_r.reshape(local_x, local_y, size_y, width_y)
    back_i = back_i.reshape(local_x, local_y, size_y, width_y)
    pieces = (
        lax.all_to_all(back_r, "qy", split_axis=2, concat_axis=1, tiled=True),
        lax.all_to_all(back_i, "qy", split_axis=2, concat_axis=1, tiled=True),
    )
    second_r, second_i = combine(cos_y, sin_y, pieces[0], pieces[1], "rq,iqak->irak")
    final_r, final_i = (
        lax.all_to_all(second_r, "qy", split_axis=1, concat_axis=2, tiled=True),
        lax.all_to_all(second_i, "qy", split_axis=1, concat_axis=2, tiled=True),
    )
    return jnp.stack(
        [final_r.reshape(local_x, local_y, entries), final_i.reshape(local_x, local_y, entries)]
    )


def solution(mesh):
    return jax.shard_map(
        per_device,
        mesh=mesh,
        in_specs=(P(None, "qx", "qy", None),),
        out_specs=P(None, "qx", "qy", None),
        check_vma=False,
    )
```

profile of v0, /device:TPU:1, one launch (start us, length us, event | category | flops | bytes accessed | tf_op | source)
XLA Modules:
  0.0 279.6 jit_solution(3963009719941379293)
XLA Ops:
  5.6 3.5 %copy.114 = f32[32,96,96]{0,2,1:T(8,128)} copy(f32[32,96,96]{2,1,0:T(8,128)S(1)} %reshape_squeeze.6) | data formatting | bytes 2359296 | tf_op jit(solution)/shard_map/reshape;squeeze | solution.py:61
  20.5 3.3 %fusion = f32[32,96,96]{2,1,0:T(8,128)S(1)} fusion(f32[32,96,96]{1,2,0:T(8,128)S(1)} %fusion.23, f32[32,96]{1,0:T(8,128)S(1)} %get-tuple-element.7, f32[96,96]{1,0:T(8,128)S(1)} %copy.113), kind=kOutput, calls=%fused_computation.1 | convolution fusion | flops 340033536 | bytes 2408448 | tf_op jit(solution)/shard_map/dot_general | solution.py:18
  26.8 3.3 %fusion.2 = f32[32,96,96]{2,1,0:T(8,128)S(1)} fusion(f32[32,96,96]{1,2,0:T(8,128)S(1)} %fusion.22, f32[32,96]{1,0:T(8,128)S(1)} %get-tuple-element.7, f32[96,96]{1,0:T(8,128)S(1)} %copy.113), kind=kOutput, calls=%fused_computation.3 | convolution fusion | flops 340033536 | bytes 2408448 | tf_op jit(solution)/shard_map/dot_general | solution.py:17
  30.1 3.4 %fusion.31 = f32[32,96,96]{2,1,0:T(8,128)S(1)} fusion(f32[32,96,96]{2,1,0:T(8,128)S(1)} %fusion, f32[32,96,96]{1,2,0:T(8,128)S(1)} %fusion.22, f32[32,96]{1,0:T(8,128)S(1)} %get-tuple-element.8, f32[96,96]{1,0:T(8,128)S(1)} %copy.113), kind=kOutput, calls=%fused_computation.35 | convolution fusion | flops 340328448 | bytes 3588096 | tf_op jit(solution)/shard_map/dot_general | solution.py:18
  33.5 3.4 %fusion.28 = f32[32,96,96]{2,1,0:T(8,128)S(1)} fusion(f32[32,96,96]{2,1,0:T(8,128)S(1)} %fusion.2, f32[32,96,96]{1,2,0:T(8,128)S(1)} %fusion.23, f32[32,96]{1,0:T(8,128)S(1)} %get-tuple-element.8, f32[96,96]{1,0:T(8,128)S(1)} %copy.113), kind=kOutput, calls=%fused_computation.34 | convolution fusion | flops 340328448 | bytes 3588096 | tf_op jit(solution)/shard_map/dot_general | solution.py:17
  51.6 3.7 %fusion.160 = f32[32,96,96]{2,1,0:T(8,128)S(1)} fusion(f32[32,96,96]{2,1,0:T(8,128)S(1)} %fusion.28, f32[32,96,96]{1,2,0:T(8,128)S(1)} %fusion.21), kind=kOutput, calls=%fused_computation.171 | convolution fusion | flops 339738624 | bytes 3538944 | tf_op jit(solution)/shard_map/dot_general | solution.py:17
  84.4 8.8 %all-to-all-start = ((f32[4,8,16,576]{3,1,0,2:T(8,128)}), f32[4,8,16,576]{3,1,0,2:T(8,128)}, u32[]{:S(2)}, u32[]{:S(2)}) async-start(f32[4,8,16,576]{3,1,0,2:T(8,128)} %copy.139), calls=%async_computation | async-start | bytes 2621440 | tf_op jit(solution)/shard_map/all_to_all | solution.py:74
  93.3 4.8 %fusion.163 = f32[32,96,96]{2,1,0:T(8,128)S(1)} fusion(f32[32,96,96]{2,1,0:T(8,128)S(1)} %copy-done.3, f32[32,96,96]{1,2,0:T(8,128)} %copy-done.4), kind=kOutput, calls=%fused_computation.174 | convolution fusion | flops 339738624 | bytes 3538944 | tf_op jit(solution)/shard_map/dot_general | solution.py:18
  98.1 3.3 %convolution_add_fusion.1 = f32[32,96,96]{2,1,0:T(8,128)S(1)} fusion(f32[32,96,96]{2,1,0:T(8,128)S(1)} %fusion.163, f32[32,96,96]{2,1,0:T(8,128)S(1)} %copy-done.1, f32[32,96,96]{1,2,0:T(8,128)S(1)} %fusion.19), kind=kOutput, calls=%fused_computation.36 | convolution fusion | flops 340033536 | bytes 4718592 | tf_op jit(solution)/shard_map/dot_general | solution.py:18
  103.4 8.7 %all-to-all-done = f32[4,8,16,576]{3,1,0,2:T(8,128)} async-done(((f32[4,8,16,576]{3,1,0,2:T(8,128)}), f32[4,8,16,576]{3,1,0,2:T(8,128)}, u32[]{:S(2)}, u32[]{:S(2)}) %all-to-all-start) | async-done | bytes 1179680 | tf_op jit(solution)/shard_map/all_to_all | solution.py:74
  112.1 5.4 %all-to-all-start.1 = ((f32[4,8,16,576]{3,1,0,2:T(8,128)}), f32[4,8,16,576]{3,1,0,2:T(8,128)S(1)}, u32[]{:S(2)}, u32[]{:S(2)}) async-start(f32[4,8,16,576]{3,1,0,2:T(8,128)} %copy.143), calls=%async_computation.1 | async-start | bytes 2621440 | tf_op jit(solution)/shard_map/all_to_all | solution.py:75
  120.3 15.8 %all-to-all-done.1 = f32[4,8,16,576]{3,1,0,2:T(8,128)S(1)} async-done(((f32[4,8,16,576]{3,1,0,2:T(8,128)}), f32[4,8,16,576]{3,1,0,2:T(8,128)S(1)}, u32[]{:S(2)}, u32[]{:S(2)}) %all-to-all-start.1) | async-done | bytes 1179680 | tf_op jit(solution)/shard_map/all_to_all | solution.py:75
  139.4 5.9 %all-to-all-start.2 = ((f32[64,8,1,576]{3,1,2,0:T(8,128)}), f32[64,8,1,576]{3,1,2,0:T(8,128)S(1)}, u32[]{:S(2)}, u32[]{:S(2)}) async-start(f32[64,8,1,576]{3,1,2,0:T(8,128)} %copy.145), calls=%async_computation.2 | async-start | bytes 2621440 | tf_op jit(solution)/shard_map/all_to_all | solution.py:79
  151.3 12.3 %all-to-all-done.2 = f32[64,8,1,576]{3,1,2,0:T(8,128)S(1)} async-done(((f32[64,8,1,576]{3,1,2,0:T(8,128)}), f32[64,8,1,576]{3,1,2,0:T(8,128)S(1)}, u32[]{:S(2)}, u32[]{:S(2)}) %all-to-all-start.2) | async-done | bytes 1179680 | tf_op jit(solution)/shard_map/all_to_all | solution.py:79
  163.6 4.8 %all-to-all-start.4 = ((f32[64,8,1,576]{3,1,2,0:T(8,128)}), f32[64,8,1,576]{3,1,2,0:T(8,128)S(1)}, u32[]{:S(2)}, u32[]{:S(2)}) async-start(f32[64,8,1,576]{3,1,2,0:T(8,128)} %copy.149), calls=%async_computation.4 | async-start | bytes 2621440 | tf_op jit(solution)/shard_map/all_to_all | solution.py:80
  173.1 12.9 %all-to-all-done.4 = f32[64,8,1,576]{3,1,2,0:T(8,128)S(1)} async-done(((f32[64,8,1,576]{3,1,2,0:T(8,128)}), f32[64,8,1,576]{3,1,2,0:T(8,128)S(1)}, u32[]{:S(2)}, u32[]{:S(2)}) %all-to-all-start.4) | async-done | bytes 1179680 | tf_op jit(solution)/shard_map/all_to_all | solution.py:80
  187.0 8.3 %all-to-all-start.3 = ((f32[4,8,8,1152]{3,1,0,2:T(8,128)}), f32[4,8,8,1152]{3,1,0,2:T(8,128)S(1)}, u32[]{:S(2)}, u32[]{:S(2)}) async-start(f32[4,8,8,1152]{3,1,0,2:T(8,128)} %copy.147), calls=%async_computation.3 | async-start | bytes 2359296 | tf_op jit(solution)/shard_map/all_to_all | solution.py:86
  201.3 10.6 %all-to-all-done.3 = f32[4,8,8,1152]{3,1,0,2:T(8,128)S(1)} async-done(((f32[4,8,8,1152]{3,1,0,2:T(8,128)}), f32[4,8,8,1152]{3,1,0,2:T(8,128)S(1)}, u32[]{:S(2)}, u32[]{:S(2)}) %all-to-all-start.3) | async-done | bytes 1179680 | tf_op jit(solution)/shard_map/all_to_all | solution.py:86
  211.9 4.3 %all-to-all-start.5 = ((f32[4,8,8,1152]{3,1,0,2:T(8,128)}), f32[4,8,8,1152]{3,1,0,2:T(8,128)S(1)}, u32[]{:S(2)}, u32[]{:S(2)}) async-start(f32[4,8,8,1152]{3,1,0,2:T(8,128)} %copy.151), calls=%async_computation.5 | async-start | bytes 2359296 | tf_op jit(solution)/shard_map/all_to_all | solution.py:87
  217.5 15.2 %all-to-all-done.5 = f32[4,8,8,1152]{3,1,0,2:T(8,128)S(1)} async-done(((f32[4,8,8,1152]{3,1,0,2:T(8,128)}), f32[4,8,8,1152]{3,1,0,2:T(8,128)S(1)}, u32[]{:S(2)}, u32[]{:S(2)}) %all-to-all-start.5) | async-done | bytes 1179680 | tf_op jit(solution)/shard_map/all_to_all | solution.py:87
  235.9 4.5 %all-to-all-start.6 = ((f32[4,64,1,1152]{3,0,2,1:T(4,128)}), f32[4,64,1,1152]{3,0,2,1:T(4,128)S(1)}, u32[]{:S(2)}, u32[]{:S(2)}) async-start(f32[4,64,1,1152]{3,0,2,1:T(4,128)} %copy.153), calls=%async_computation.6 | async-start | bytes 2359296 | tf_op jit(solution)/shard_map/all_to_all | solution.py:91
  244.8 12.0 %all-to-all-done.6 = f32[4,64,1,1152]{3,0,2,1:T(4,128)S(1)} async-done(((f32[4,64,1,1152]{3,0,2,1:T(4,128)}), f32[4,64,1,1152]{3,0,2,1:T(4,128)S(1)}, u32[]{:S(2)}, u32[]{:S(2)}) %all-to-all-start.6) | async-done | bytes 1179680 | tf_op jit(solution)/shard_map/all_to_all | solution.py:91
  256.9 4.3 %all-to-all-start.7 = ((f32[4,64,1,1152]{3,0,2,1:T(4,128)}), f32[4,64,1,1152]{3,0,2,1:T(4,128)S(1)}, u32[]{:S(2)}, u32[]{:S(2)}) async-start(f32[4,64,1,1152]{3,0,2,1:T(4,128)} %copy.155), calls=%async_computation.7 | async-start | bytes 2359296 | tf_op jit(solution)/shard_map/all_to_all | solution.py:92
  261.3 16.4 %all-to-all-done.7 = f32[4,64,1,1152]{3,0,2,1:T(4,128)S(1)} async-done(((f32[4,64,1,1152]{3,0,2,1:T(4,128)}), f32[4,64,1,1152]{3,0,2,1:T(4,128)S(1)}, u32[]{:S(2)}, u32[]{:S(2)}) %all-to-all-start.7) | async-done | bytes 1179680 | tf_op jit(solution)/shard_map/all_to_all | solution.py:92
  (66 shorter events, 99.9 us)
Async XLA Ops:
  58.6 18.1 %copy-start = (f32[32,96,96]{2,1,0:T(8,128)}, f32[32,96,96]{2,1,0:T(8,128)S(1)}, u32[]{:S(2)}) copy-start(f32[32,96,96]{2,1,0:T(8,128)S(1)} %convolution_add_fusion.2) | copy-start | bytes 3538948
  61.9 11.4 %copy-start.2 = (f32[32,96,96]{2,1,0:T(8,128)}, f32[32,96,96]{2,1,0:T(8,128)S(1)}, u32[]{:S(2)}) copy-start(f32[32,96,96]{2,1,0:T(8,128)S(1)} %convolution_subtract_fusion.2) | copy-start | bytes 3538948
  73.3 3.3 %copy-start.4 = (f32[32,96,96]{1,2,0:T(8,128)}, f32[32,96,96]{1,2,0:T(8,128)S(1)}, u32[]{:S(2)}) copy-start(f32[32,96,96]{1,2,0:T(8,128)S(1)} %fusion.18) | copy-start | bytes 3538948
  84.4 8.8 %copy-start.3 = (f32[32,96,96]{2,1,0:T(8,128)S(1)}, f32[32,96,96]{2,1,0:T(8,128)}, u32[]{:S(2)}) copy-start(f32[32,96,96]{2,1,0:T(8,128)} %copy-done.2) | copy-start | bytes 3538948
  84.4 27.7 %all-to-all-start = ((f32[4,8,16,576]{3,1,0,2:T(8,128)}), f32[4,8,16,576]{3,1,0,2:T(8,128)}, u32[]{:S(2)}, u32[]{:S(2)}) async-start(f32[4,8,16,576]{3,1,0,2:T(8,128)} %copy.139), calls=%async_computation | async-start | bytes 2621440 | tf_op jit(solution)/shard_map/all_to_all | solution.py:74
  93.2 4.8 %copy-start.1 = (f32[32,96,96]{2,1,0:T(8,128)S(1)}, f32[32,96,96]{2,1,0:T(8,128)}, u32[]{:S(2)}) copy-start(f32[32,96,96]{2,1,0:T(8,128)} %copy-done) | copy-start | bytes 3538948
  112.1 24.0 %all-to-all-start.1 = ((f32[4,8,16,576]{3,1,0,2:T(8,128)}), f32[4,8,16,576]{3,1,0,2:T(8,128)S(1)}, u32[]{:S(2)}, u32[]{:S(2)}) async-start(f32[4,8,16,576]{3,1,0,2:T(8,128)} %copy.143), calls=%async_computation.1 | async-start | bytes 2621440 | tf_op jit(solution)/shard_map/all_to_all | solution.py:75
  139.4 24.3 %all-to-all-start.2 = ((f32[64,8,1,576]{3,1,2,0:T(8,128)}), f32[64,8,1,576]{3,1,2,0:T(8,128)S(1)}, u32[]{:S(2)}, u32[]{:S(2)}) async-start(f32[64,8,1,576]{3,1,2,0:T(8,128)} %copy.145), calls=%async_computation.2 | async-start | bytes 2621440 | tf_op jit(solution)/shard_map/all_to_all | solution.py:79
  163.6 22.3 %all-to-all-start.4 = ((f32[64,8,1,576]{3,1,2,0:T(8,128)}), f32[64,8,1,576]{3,1,2,0:T(8,128)S(1)}, u32[]{:S(2)}, u32[]{:S(2)}) async-start(f32[64,8,1,576]{3,1,2,0:T(8,128)} %copy.149), calls=%async_computation.4 | async-start | bytes 2621440 | tf_op jit(solution)/shard_map/all_to_all | solution.py:80
  186.0 1.1 copy-start.5
  187.0 24.8 %all-to-all-start.3 = ((f32[4,8,8,1152]{3,1,0,2:T(8,128)}), f32[4,8,8,1152]{3,1,0,2:T(8,128)S(1)}, u32[]{:S(2)}, u32[]{:S(2)}) async-start(f32[4,8,8,1152]{3,1,0,2:T(8,128)} %copy.147), calls=%async_computation.3 | async-start | bytes 2359296 | tf_op jit(solution)/shard_map/all_to_all | solution.py:86
  211.9 20.9 %all-to-all-start.5 = ((f32[4,8,8,1152]{3,1,0,2:T(8,128)}), f32[4,8,8,1152]{3,1,0,2:T(8,128)S(1)}, u32[]{:S(2)}, u32[]{:S(2)}) async-start(f32[4,8,8,1152]{3,1,0,2:T(8,128)} %copy.151), calls=%async_computation.5 | async-start | bytes 2359296 | tf_op jit(solution)/shard_map/all_to_all | solution.py:87
  235.9 21.0 %all-to-all-start.6 = ((f32[4,64,1,1152]{3,0,2,1:T(4,128)}), f32[4,64,1,1152]{3,0,2,1:T(4,128)S(1)}, u32[]{:S(2)}, u32[]{:S(2)}) async-start(f32[4,64,1,1152]{3,0,2,1:T(4,128)} %copy.153), calls=%async_computation.6 | async-start | bytes 2359296 | tf_op jit(solution)/shard_map/all_to_all | solution.py:91
  256.9 20.9 %all-to-all-start.7 = ((f32[4,64,1,1152]{3,0,2,1:T(4,128)}), f32[4,64,1,1152]{3,0,2,1:T(4,128)S(1)}, u32[]{:S(2)}, u32[]{:S(2)}) async-start(f32[4,64,1,1152]{3,0,2,1:T(4,128)} %copy.155), calls=%async_computation.7 | async-start | bytes 2359296 | tf_op jit(solution)/shard_map/all_to_all | solution.py:92
where the time goes:
time: 283 us; the launch traced here: 280 us
  waiting for transfers between devices  104 us (37%)
  matrix products  89.5 us (32%)
  starting transfers between devices  46.5 us (16%)
  local copies, waits for them, and re-layouts  37.4 us (13%)
    dot_general x6, matrix products, cmatmul(): jnp.matmul(ar, bi, precision=hp) + jnp.matmul(ai, br, precision=hp)  20 us
    dot_general x6, matrix products, cmatmul(): jnp.matmul(ar, br, precision=hp) - jnp.matmul(ai, bi, precision=hp)  18.7 us
    dot_general x6, matrix products, cmatmul(): jnp.matmul(ai, br, precision=hp)  18.6 us
    dot_general x6, matrix products, cmatmul(): jnp.matmul(ai, bi, precision=hp)  18.5 us
    all_to_all x1, waiting for transfers between devices, per_device(): lax.all_to_all(second_i, 'qy', split_axis=1, concat_axis=2, tiled=True)  16.4 us
    all_to_all x1, waiting for transfers between devices, per_device(): lax.all_to_all(part_i, 'qx', split_axis=2, concat_axis=0, tiled=True)  15.8 us
    all_to_all x1, waiting for transfers between devices, per_device(): lax.all_to_all(back_i, 'qy', split_axis=2, concat_axis=1, tiled=True)  15.2 us
    all_to_all x1, waiting for transfers between devices, per_device(): lax.all_to_all(first_i, 'qx', split_axis=0, concat_axis=2, tiled=True)  12.9 us
  transfers between devices with their start and end apart: 8, of which 8 were waited for; matrix products, arithmetic and copies ran while one was open for 13% of the time, Pallas kernels for 0%

commit v1 on v0

v1 whole, which is shorter than its diff:
```python
import functools

import jax
import jax.numpy as jnp
import ml_dtypes
import numpy as np
from jax import lax
from jax.experimental import pallas as pl
from jax.experimental.pallas import tpu as pltpu
from jax.sharding import PartitionSpec as P

M = 96
ETA = 0.25
NDEV = 128
SIZE_X, SIZE_Y = 16, 8
LOCAL_X, LOCAL_Y = 4, 8
Q = LOCAL_X * LOCAL_Y
L = 128
ROWS = (8, 10)
PITCH = (16, 24)
USED = (16, 20)
MESH = pl.DeviceIdType.MESH
F32 = jnp.float32
BF16 = jnp.bfloat16


def split_table(table):
    high = table.astype(ml_dtypes.bfloat16)
    low = (table - high.astype(np.float64)).astype(ml_dtypes.bfloat16)
    return high, low


def embed_table(angle):
    cosine, sine = np.cos(angle), np.sin(angle)
    return np.block([[cosine, -sine], [sine, cosine]])


def tables():
    ax, ay = np.divmod(np.arange(NDEV), SIZE_Y)
    turns = (ax[:, None] * ax[None, :] % 16) / 16 + (ay[:, None] * ay[None, :] % 8) / 8
    first = np.concatenate(split_table(embed_table(2 * np.pi * turns)), axis=0)
    lane = np.arange(L)
    bx, by = lane % Q // LOCAL_Y, lane % LOCAL_Y
    turns = (ax[:, None] * bx[None, :] + ay[:, None] * by[None, :]) / 64
    twiddle = np.stack([np.cos(2 * np.pi * turns), np.sin(2 * np.pi * turns)]) / 64
    turns = (bx[:, None] * bx[None, :] % 4) / 4 + (by[:, None] * by[None, :] % 8) / 8
    same = (lane[:, None] // Q) == (lane[None, :] // Q)
    angle = 2 * np.pi * turns
    cosine, sine = np.cos(angle) * same, np.sin(angle) * same
    second = np.concatenate(split_table(np.block([[cosine, -sine], [sine, cosine]])), axis=0)
    return first, twiddle.astype(np.float32), second


def split(value):
    high = value.astype(BF16)
    low = (value - high.astype(F32)).astype(BF16)
    return high, low


def dot(a, b, contract=0):
    return lax.dot_general(a, b, (((1,), (contract,)), ((), ())), preferred_element_type=F32)


def embed(part):
    zeros = jnp.zeros((L - M, 2 * L), part.dtype)
    real, imag = part[:, :L], part[:, L:]
    return jnp.concatenate(
        [part, zeros, jnp.concatenate([-imag, real], axis=1), zeros], axis=0
    )


def product(left, right):
    n = left[0].shape[0]
    both = dot(jnp.concatenate(left, axis=0), embed(right[0]))
    return both[:n] + both[n:] + dot(left[0], embed(right[1]))


def invert(real, imag):
    row = lax.broadcasted_iota(jnp.int32, (M, L), 0)
    col = lax.broadcasted_iota(jnp.int32, (M, L), 1)
    eye = row == col
    off = (col < M) & (row != col)
    diag = jnp.where(eye, real, 0.0)

    def start(d):
        denom = d * d + ETA * ETA
        return d / denom, -ETA / denom

    cr, ci = start(jnp.sum(diag, axis=0, keepdims=True))
    rr, ri = start(jnp.sum(diag, axis=1, keepdims=True))
    er = jnp.where(off, imag * ci - real * cr, 0.0)
    ei = jnp.where(off, -(real * ci + imag * cr), 0.0)
    pr = jnp.where(eye, 1.0, er)
    x1 = jnp.concatenate([rr * pr - ri * ei, rr * ei + ri * pr], axis=1)
    e0 = split(jnp.concatenate([er, ei], axis=1))
    e1 = product(e0, e0)
    e1s = split(e1)
    x1s = split(x1)
    both = product(
        (jnp.concatenate([x1s[0], e1s[0]], axis=0), jnp.concatenate([x1s[1], e1s[1]], axis=0)), e1s
    )
    x2 = x1 + both[:M]
    return x2 + product(split(x2), split(both[M:]))


def kernel(
    d_ref, first_ref, twiddle_ref, second_ref, out_ref,
    mat, s0, s1, r0, r1, t0, t1, v0, v1, up_h, up_l, ssem, rsem, osem,
):
    qx = lax.axis_index("qx")
    qy = lax.axis_index("qy")
    me = qx * SIZE_Y + qy

    barrier = pltpu.get_barrier_semaphore()

    def greet(o, carry):
        other = lax.rem(me + o, NDEV)
        pl.semaphore_signal(
            barrier, inc=1, device_id=(other // SIZE_Y, lax.rem(other, SIZE_Y)), device_id_type=MESH
        )
        return carry

    lax.fori_loop(1, NDEV, greet, 0)

    def unflatten(n, carry):
        part, x = n // LOCAL_X, lax.rem(n, LOCAL_X)
        for i in range(M):
            first, last = i * M // L, min((i * M + L - 1) // L, 71)
            off = i * M % L
            tile = d_ref[part, x, :, first * L : (first + 1) * L]
            if off:
                lane = lax.broadcasted_iota(jnp.int32, (LOCAL_Y, L), 1)
                tile = pltpu.roll(tile, L - off, 1)
                if last > first:
                    after = pltpu.roll(d_ref[part, x, :, last * L : (last + 1) * L], L - off, 1)
                    tile = jnp.where(lane < L - off, tile, after)
            mat[part, pl.ds(x * LOCAL_Y * M + i, LOCAL_Y, stride=M), :] = tile
        return carry

    lax.fori_loop(0, 2 * LOCAL_X, unflatten, 0)

    def invert_one(n, carry):
        for k in range(2):
            rows = pl.ds(pl.multiple_of((2 * n + k) * M, M), M)
            result = invert(mat[0, rows, :], mat[1, rows, :])
            mat[0, rows, :] = result[:, :L]
            mat[1, rows, :] = result[:, L:]
        return carry

    lax.fori_loop(0, Q // 2, invert_one, 0)

    sends = (s0, s1)
    lands = (r0, r1)
    outs = (t0, t1)
    backs = (v0, v1)

    def exchange(src, dst, c, phase):
        used = pl.ds(0, USED[c])
        own = pltpu.make_async_copy(src.at[me, used], dst.at[me, used], rsem.at[phase, c])
        own.start()

        def send(o, carry):
            k = lax.rem(o, 4)
            core, a, b = lax.rem(o // 4, 2), lax.rem(o // 8, 4), o // 32
            z, x = qx // 4, lax.rem(qx, 4)
            y, h = qy // 2, lax.rem(qy, 2)
            tx = lax.rem(z + k, 4) * 4 + lax.rem(x + k + a, 4)
            ty = lax.rem(y + k + b, 4) * 2 + lax.rem(h + core, 2)
            target = tx * SIZE_Y + ty

            @pl.when(target != me)
            def _():
                pltpu.make_async_remote_copy(
                    src_ref=src.at[target, used],
                    dst_ref=dst.at[me, used],
                    send_sem=ssem.at[phase, c],
                    recv_sem=rsem.at[phase, c],
                    device_id=(tx, ty),
                    device_id_type=MESH,
                ).start()

            return carry

        lax.fori_loop(0, NDEV, send, 0)

    def arrived(dst, c, phase):
        whole = dst.at[:, pl.ds(0, USED[c])]
        pltpu.make_async_copy(whole, whole, rsem.at[phase, c]).wait()

    def sent(src, c, phase):
        whole = src.at[pl.ds(0, NDEV - 1), pl.ds(0, USED[c])]
        pltpu.make_async_copy(whole, whole, ssem.at[phase, c]).wait()

    def flat(ref, c):
        return ref.reshape(NDEV * PITCH[c], L)

    def pack(c, part, u, v, first_row):
        block = jnp.concatenate(
            [
                mat[part, pl.ds(16 * u + 4 * g + v, Q, stride=M), :]
                for g in range(4)
            ],
            axis=0,
        ).T
        for w in range(3):
            lo, hi = max(0, w * L - v * M), min(M, (w + 1) * L - v * M)
            if lo >= hi:
                continue
            row = 3 * u + w
            c = 0 if row < ROWS[0] else 1
            local = part * ROWS[c] + row - (0 if c == 0 else ROWS[0])
            target = v * M + lo - w * L
            flat(sends[c], c)[pl.ds(target * PITCH[c] + local, hi - lo, stride=PITCH[c]), :] = block[lo:hi]

    for u in range(6):
        for v in range(4):
            for part in range(2):
                pack(0, part, u, v, 0)
        if u == 2:
            pl.semaphore_wait(barrier, NDEV - 1)
            exchange(s0, r0, 0, 0)
    exchange(s1, r1, 1, 0)

    def stage_one(c, pair):
        src = flat(lands[c], c)
        cols = []
        for row in (2 * pair, 2 * pair + 1):
            cols.append(
                jnp.concatenate(
                    [src[pl.ds(part * ROWS[c] + row, NDEV, stride=PITCH[c]), :] for part in range(2)],
                    axis=0,
                )
            )
        high, low = split(jnp.concatenate(cols, axis=1))
        table = first_ref[...]
        both = dot(table, high)
        total = both[: 2 * L] + both[2 * L :] + dot(table[: 2 * L], low)
        tr, ti = twiddle_ref[0], twiddle_ref[1]
        for k in range(2):
            real, imag = total[:L, k * L : (k + 1) * L], total[L:, k * L : (k + 1) * L]
            yield jnp.concatenate([real * tr - imag * ti, real * ti + imag * tr], axis=1)

    def stage_two(c0, n):
        high, low = up_h[c0], up_l[c0]
        table = second_ref[...]
        both = dot(table, high, 1)
        return both[: 2 * L] + both[2 * L :] + dot(table[: 2 * L], low, 1)

    def transform(c):
        for pair in range(4):
            for k, rows in enumerate(stage_one(c, pair)):
                high, low = split(rows)
                row = 2 * pair + k
                for c0 in range(4):
                    up_h[c0, row * Q : (row + 1) * Q, :] = high[c0 * Q : (c0 + 1) * Q]
                    up_l[c0, row * Q : (row + 1) * Q, :] = low[c0 * Q : (c0 + 1) * Q]
        dst = flat(outs[c], c)
        for c0 in range(4):
            result = stage_two(c0, 0)
            for part in range(2):
                for g in range(4):
                    for jx in range(4):
                        r = part * L + g * Q + jx * 8
                        for quad in range(2):
                            dst[
                                pl.ds((4 * jx + c0) * 8 * PITCH[c] + part * 8 + g * 2 + quad, 8, stride=PITCH[c]), :
                            ] = result[r : r + 8, quad * L : (quad + 1) * L]
        if c == 0:
            return
        for k, rows in enumerate(stage_one(c, 4)):
            high, low = split(rows)
            for c0 in range(4):
                at = c0 * 2 * Q + k * Q
                up_h[0, at : at + Q, :] = high[c0 * Q : (c0 + 1) * Q]
                up_l[0, at : at + Q, :] = low[c0 * Q : (c0 + 1) * Q]
        result = stage_two(0, 0)
        lane = lax.broadcasted_iota(jnp.int32, (8, L), 1)
        for c0 in range(4):
            col = c0 // 2 * L
            for part in range(2):
                for gh in range(2):
                    for jx in range(4):
                        r = part * L + gh * 2 * Q + jx * 8
                        one = result[r : r + 8, col : col + L]
                        two = result[r + Q : r + Q + 8, col : col + L]
                        if c0 % 2 == 0:
                            row = jnp.where(lane < 64, one, pltpu.roll(two, 64, 1))
                        else:
                            row = jnp.where(lane < 64, pltpu.roll(one, 64, 1), two)
                        dst[
                            pl.ds((4 * jx + c0) * 8 * PITCH[c] + 16 + part * 2 + gh, 8, stride=PITCH[c]), :
                        ] = row

    def place(part, g, row, block):
        tile = 12 * (row // 3) + 3 * g + row % 3
        out_ref[part, :, :, tile * L : (tile + 1) * L] = block.reshape(LOCAL_X, LOCAL_Y, L)

    def finish(c):
        src = flat(backs[c], c)
        for part in range(2):
            for g in range(4):
                for quad in range(2):
                    block = src[pl.ds(part * 8 + g * 2 + quad, NDEV, stride=PITCH[c]), :].T
                    for k in range(4):
                        place(part, g, 8 * c + 4 * quad + k, block[k * Q : (k + 1) * Q])
            if c == 1:
                for gh in range(2):
                    block = src[pl.ds(16 + part * 2 + gh, NDEV, stride=PITCH[c]), :].T
                    for gl in range(2):
                        for k in range(2):
                            at = (2 * gl + k) * Q
                            place(part, 2 * gh + gl, 16 + k, block[at : at + Q])

    for c in range(2):
        arrived(lands[c], c, 0)
        transform(c)
        exchange(outs[c], backs[c], c, 1)
    for c in range(2):
        arrived(backs[c], c, 1)
        finish(c)
    for c in range(2):
        sent(sends[c], c, 0)
        sent(outs[c], c, 1)


def per_device(dynamical):
    vmem = pl.BlockSpec(memory_space=pltpu.VMEM)
    buffers = [pltpu.VMEM((NDEV, p, L), F32) for p in PITCH]
    return pl.pallas_call(
        kernel,
        out_shape=jax.ShapeDtypeStruct(dynamical.shape, F32),
        in_specs=[vmem] * 4,
        out_specs=vmem,
        scratch_shapes=[
            pltpu.VMEM((2, Q * M, L), F32),
            *buffers, *buffers, *buffers, *buffers,
            pltpu.VMEM((4, 2 * L, 2 * L), BF16),
            pltpu.VMEM((4, 2 * L, 2 * L), BF16),
            pltpu.SemaphoreType.DMA((2, 2)),
            pltpu.SemaphoreType.DMA((2, 2)),
            pltpu.SemaphoreType.REGULAR,
        ],
        compiler_params=pltpu.CompilerParams(
            collective_id=0, has_side_effects=True, vmem_limit_bytes=48 << 20
        ),
    )(dynamical, *tables())


def solution(mesh):
    return jax.shard_map(
        per_device,
        mesh=mesh,
        in_specs=(P(None, "qx", "qy", None),),
        out_specs=P(None, "qx", "qy", None),
        check_vma=False,
    )
```

time: 283 us -> 92.1 us (0.33)
  waiting for transfers between devices: 104 us -> 0 us
  matrix products: 89.5 us -> 0 us
  Pallas kernels: 0 us -> 85.5 us
  starting transfers between devices: 46.5 us -> 0 us
  local copies, waits for them, and re-layouts: 37.4 us -> 5.88 us
    all_to_all x8 -> x0, waiting for transfers between devices: 104 us -> none  [the longest x1 16.4 us: per_device(): lax.all_to_all(second_i, 'qy', split_axis=1, concat_axis=2, tiled=True)]
    dot_general x32 -> x0, matrix products: 89.5 us -> none  [the longest x6 20 us: cmatmul(): jnp.matmul(ar, bi, precision=hp) + jnp.matmul(ai, br, precision=hp)]
    pallas_call x0 -> x1, Pallas kernels: none -> 85.5 us  [per_device(): pl.pallas_call(kernel, out_shape=jax.ShapeDtypeStruct(dynamical.shape, F3...]
    all_to_all x8 -> x0, starting transfers between devices: 46.5 us -> none  [the longest x1 8.83 us: per_device(): lax.all_to_all(part_r, 'qx', split_axis=2, concat_axis=0, tiled=True)]
    reshape x8 -> x0, local copies, waits for them, and re-layouts: 13.1 us -> none  [the longest x2 4.44 us: per_device(): part_r = xr.reshape(local_x, local_y, size_x, width_x)]
    another operation x3 -> x0, local copies, waits for them, and re-layouts: 5.97 us -> none  [the longest x2 4.07 us: per_device(): real_in = dynamical[0].reshape(count, M, M)]
    unnamed x12 -> x9, local copies, waits for them, and re-layouts: 1.08 us -> 5.88 us
    all_to_all x4 -> x0, local copies, waits for them, and re-layouts: 4.05 us -> none  [the longest x1 2.08 us: per_device(): lax.all_to_all(first_i, 'qx', split_axis=0, concat_axis=2, tiled=True)]
  transfers between devices with their start and end apart: 8 -> 0, of which waited for: 8 -> 0; matrix products, arithmetic and copies ran while one was open for 13% -> 0% of each run, Pallas kernels for 0% -> 0%
where the time goes in v1:
time: 92.1 us; the launch traced here: 91.4 us
  Pallas kernels  85.5 us (93%)
  local copies, waits for them, and re-layouts  5.88 us (6%)
    pallas_call x1, Pallas kernels, per_device(): pl.pallas_call(kernel, out_shape=jax.ShapeDtypeStruct(dynamical.shape, F3...  85.5 us
    unnamed x9, local copies, waits for them, and re-layouts  5.88 us

profile of v1, /device:TPU:1, one launch (start us, length us, event | category | flops | bytes accessed | tf_op | source)
XLA Modules:
  0.0 91.4 jit_solution(1131404087758370257)
XLA Ops:
  0.0 0.0 copy-start
  0.0 1.7 %copy-done = f32[2,4,8,9216]{3,2,1,0:T(8,128)S(1)} copy-done((f32[2,4,8,9216]{3,2,1,0:T(8,128)S(1)}, f32[2,4,8,9216]{3,2,1,0:T(8,128)}, u32[]{:S(2)}) %copy-start) | copy-done | bytes 2359320
  1.7 0.0 copy-start.1
  1.7 0.9 %copy-done.1 = bf16[512,256]{1,0:T(8,128)(2,1)S(1)} copy-done((bf16[512,256]{1,0:T(8,128)(2,1)S(1)}, bf16[512,256]{1,0:T(8,128)(2,1)}, u32[]{:S(2)}) %copy-start.1) | copy-done | bytes 262168
  2.6 0.0 copy-start.2
  2.6 0.9 %copy-done.2 = bf16[512,256]{1,0:T(8,128)(2,1)S(1)} copy-done((bf16[512,256]{1,0:T(8,128)(2,1)S(1)}, bf16[512,256]{1,0:T(8,128)(2,1)}, u32[]{:S(2)}) %copy-start.2) | copy-done | bytes 262168
  3.6 0.0 copy-start.3
  3.6 0.9 copy-done.3
  4.5 85.5 %shard_map.46 = f32[2,4,8,9216]{3,2,1,0:T(8,128)S(1)} custom-call(f32[2,4,8,9216]{3,2,1,0:T(8,128)S(1)} %copy-done, bf16[512,256]{1,0:T(8,128)(2,1)S(1)} %copy-done.2, f32[2,128,128]{2,1,0:T(8,128)S(1)} %copy-done.3, bf16[512,256]{1,0:T(8,128)(2,1)S(1)} %copy-done.1), custom_call_target="tpu_custom_call" | custom-call | tf_op jit(solution)/shard_map/pallas_call | solution.py:329
  90.0 1.4 %copy.6 = f32[2,4,8,9216]{3,2,1,0:T(8,128)} copy(f32[2,4,8,9216]{3,2,1,0:T(8,128)S(1)} %shard_map.46) | data formatting | bytes 4718592
Async XLA Ops:
  0.0 1.7 %copy-start = (f32[2,4,8,9216]{3,2,1,0:T(8,128)S(1)}, f32[2,4,8,9216]{3,2,1,0:T(8,128)}, u32[]{:S(2)}) copy-start(f32[2,4,8,9216]{3,2,1,0:T(8,128)} %d_ref.1) | copy-start | bytes 7077892
  1.7 0.9 %copy-start.1 = (bf16[512,256]{1,0:T(8,128)(2,1)S(1)}, bf16[512,256]{1,0:T(8,128)(2,1)}, u32[]{:S(2)}) copy-start(bf16[512,256]{1,0:T(8,128)(2,1)} %constant.8.clone.second_ref) | copy-start | bytes 786436
  2.6 0.9 %copy-start.2 = (bf16[512,256]{1,0:T(8,128)(2,1)S(1)}, bf16[512,256]{1,0:T(8,128)(2,1)}, u32[]{:S(2)}) copy-start(bf16[512,256]{1,0:T(8,128)(2,1)} %constant.6.clone.first_ref) | copy-start | bytes 786436
  3.6 0.9 copy-start.3

commit v2 on v1

--- a/solution.py
+++ b/solution.py
@@ -75,7 +75,7 @@
     return both[:n] + both[n:] + dot(left[0], embed(right[1]))
 
 
-def invert(real, imag):
+def begin(real, imag):
     row = lax.broadcasted_iota(jnp.int32, (M, L), 0)
     col = lax.broadcasted_iota(jnp.int32, (M, L), 1)
     eye = row == col
@@ -92,62 +92,78 @@
     ei = jnp.where(off, -(real * ci + imag * cr), 0.0)
     pr = jnp.where(eye, 1.0, er)
     x1 = jnp.concatenate([rr * pr - ri * ei, rr * ei + ri * pr], axis=1)
-    e0 = split(jnp.concatenate([er, ei], axis=1))
-    e1 = product(e0, e0)
-    e1s = split(e1)
-    x1s = split(x1)
-    both = product(
-        (jnp.concatenate([x1s[0], e1s[0]], axis=0), jnp.concatenate([x1s[1], e1s[1]], axis=0)), e1s
-    )
-    x2 = x1 + both[:M]
-    return x2 + product(split(x2), split(both[M:]))
+    return x1, split(jnp.concatenate([er, ei], axis=1))
+
+
+def stack(a, b):
+    return tuple(jnp.concatenate(pair, axis=0) for pair in zip(a, b))
+
+
+def invert(matrices):
+    x1, e0 = zip(*[begin(*m) for m in matrices])
+    e1 = [split(product(e, e)) for e in e0]
+    both = [product(stack(split(x), e), e) for x, e in zip(x1, e1)]
+    x2 = [x + b[:M] for x, b in zip(x1, both)]
+    return [x + product(split(x), split(b[M:])) for x, b in zip(x2, both)]
 
 
 def kernel(
+    d_hbm, first_hbm, twiddle_hbm, second_hbm, out_hbm,
     d_ref, first_ref, twiddle_ref, second_ref, out_ref,
-    mat, s0, s1, r0, r1, t0, t1, v0, v1, up_h, up_l, ssem, rsem, osem,
+    mat, s0, s1, r0, r1, t0, t1, v0, v1, up_h, up_l, ssem, rsem, dsem, csem, osem,
 ):
     qx = lax.axis_index("qx")
     qy = lax.axis_index("qy")
     me = qx * SIZE_Y + qy
 
+    def fetch(x):
+        return pltpu.make_async_copy(d_hbm.at[:, x], d_ref.at[:, x], dsem.at[x])
+
+    for x in range(LOCAL_X):
+        fetch(x).start()
+    constants = [
+        pltpu.make_async_copy(first_hbm, first_ref, csem.at[0]),
+        pltpu.make_async_copy(twiddle_hbm, twiddle_ref, csem.at[1]),
+        pltpu.make_async_copy(second_hbm, second_ref, csem.at[2]),
+    ]
+    for copy in constants:
+        copy.start()
+
     barrier = pltpu.get_barrier_semaphore()
 
-    def greet(o, carry):
-        other = lax.rem(me + o, NDEV)
+    def greet(o):
+        other = jnp.bitwise_xor(me, o)
         pl.semaphore_signal(
-            barrier, inc=1, device_id=(other // SIZE_Y, lax.rem(other, SIZE_Y)), device_id_type=MESH
+            barrier, inc=1, device_id=(other >> 3, other & 7), device_id_type=MESH
         )
+
+    for o in range(1, 4):
+        greet(o)
+
+    def invert_some(x, carry):
+        fetch(x).wait()
+        lane = lax.broadcasted_iota(jnp.int32, (LOCAL_Y, L), 1)
+        base = x * (LOCAL_Y * M)
+        for part in range(2):
+            for i in range(M):
+                tile, off = divmod(i * M, L)
+                row = d_ref[part, x, :, tile * L : (tile + 1) * L]
+                if off:
+                    row = pltpu.roll(row, L - off, 1)
+                if off + M > L:
+                    after = d_ref[part, x, :, (tile + 1) * L : (tile + 2) * L]
+                    row = jnp.where(lane < L - off, row, pltpu.roll(after, L - off, 1))
+                mat[part, pl.ds(base + i, LOCAL_Y, stride=M), :] = row
+        for o in range(31):
+            greet(4 + x * 31 + o)
+        rows = [pl.ds(pl.multiple_of(base + k * M, M), M) for k in range(LOCAL_Y)]
+        results = invert([(mat[0, r, :], mat[1, r, :]) for r in rows])
+        for r, result in zip(rows, results):
+            mat[0, r, :] = result[:, :L]
+            mat[1, r, :] = result[:, L:]
         return carry
 
-    lax.fori_loop(1, NDEV, greet, 0)
-
-    def unflatten(n, carry):
-        part, x = n // LOCAL_X, lax.rem(n, LOCAL_X)
-        for i in range(M):
-            first, last = i * M // L, min((i * M + L - 1) // L, 71)
-            off = i * M % L
-            tile = d_ref[part, x, :, first * L : (first + 1) * L]
-            if off:
-                lane = lax.broadcasted_iota(jnp.int32, (LOCAL_Y, L), 1)
-                tile = pltpu.roll(tile, L - off, 1)
-                if last > first:
-                    after = pltpu.roll(d_ref[part, x, :, last * L : (last + 1) * L], L - off, 1)
-                    tile = jnp.where(lane < L - off, tile, after)
-            mat[part, pl.ds(x * LOCAL_Y * M + i, LOCAL_Y, stride=M), :] = tile
-        return carry
-
-    lax.fori_loop(0, 2 * LOCAL_X, unflatten, 0)
-
-    def invert_one(n, carry):
-        for k in range(2):
-            rows = pl.ds(pl.multiple_of((2 * n + k) * M, M), M)
-            result = invert(mat[0, rows, :], mat[1, rows, :])
-            mat[0, rows, :] = result[:, :L]
-            mat[1, rows, :] = result[:, L:]
-        return carry
-
-    lax.fori_loop(0, Q // 2, invert_one, 0)
+    lax.fori_loop(0, LOCAL_X, invert_some, 0)
 
     sends = (s0, s1)
     lands = (r0, r1)
@@ -160,28 +176,30 @@
         own.start()
 
         def send(o, carry):
-            k = lax.rem(o, 4)
-            core, a, b = lax.rem(o // 4, 2), lax.rem(o // 8, 4), o // 32
-            z, x = qx // 4, lax.rem(qx, 4)
-            y, h = qy // 2, lax.rem(qy, 2)
-            tx = lax.rem(z + k, 4) * 4 + lax.rem(x + k + a, 4)
-            ty = lax.rem(y + k + b, 4) * 2 + lax.rem(h + core, 2)
-            target = tx * SIZE_Y + ty
-
-            @pl.when(target != me)
-            def _():
-                pltpu.make_async_remote_copy(
-                    src_ref=src.at[target, used],
-                    dst_ref=dst.at[me, used],
-                    send_sem=ssem.at[phase, c],
-                    recv_sem=rsem.at[phase, c],
-                    device_id=(tx, ty),
-                    device_id_type=MESH,
-                ).start()
-
+            z, x, y, h = qx >> 2, (qx & 3) + (o & 3), (qy >> 1) + (o >> 2), qy & 1
+            for n in range(8):
+                k, core = n & 3, n >> 2
+                tx = (((z + k) & 3) << 2) | ((x + k) & 3)
+                ty = (((y + k) & 3) << 1) | (h ^ core)
+                target = (tx << 3) | ty
+
+                def start():
+                    pltpu.make_async_remote_copy(
+                        src_ref=src.at[target, used],
+                        dst_ref=dst.at[me, used],
+                        send_sem=ssem.at[phase, c],
+                        recv_sem=rsem.at[phase, c],
+                        device_id=(tx, ty),
+                        device_id_type=MESH,
+                    ).start()
+
+                if n == 0:
+                    pl.when(target != me)(start)
+                else:
+                    start()
             return carry
 
-        lax.fori_loop(0, NDEV, send, 0)
+        lax.fori_loop(0, NDEV // 8, send, 0)
 
     def arrived(dst, c, phase):
         whole = dst.at[:, pl.ds(0, USED[c])]
@@ -291,59 +309,82 @@
                             pl.ds((4 * jx + c0) * 8 * PITCH[c] + 16 + part * 2 + gh, 8, stride=PITCH[c]), :
                         ] = row
 
+    def write(tile, tiles):
+        part = pl.ds(tile * L, tiles * L)
+        return pltpu.make_async_copy(out_ref.at[:, :, :, part], out_hbm.at[:, :, :, part], osem.at[tile // 24])
+
     def place(part, g, row, block):
         tile = 12 * (row // 3) + 3 * g + row % 3
         out_ref[part, :, :, tile * L : (tile + 1) * L] = block.reshape(LOCAL_X, LOCAL_Y, L)
 
-    def finish(c):
+    def finish(c, quad):
         src = flat(backs[c], c)
         for part in range(2):
             for g in range(4):
-                for quad in range(2):
-                    block = src[pl.ds(part * 8 + g * 2 + quad, NDEV, stride=PITCH[c]), :].T
-                    for k in range(4):
-                        place(part, g, 8 * c + 4 * quad + k, block[k * Q : (k + 1) * Q])
-            if c == 1:
-                for gh in range(2):
-                    block = src[pl.ds(16 + part * 2 + gh, NDEV, stride=PITCH[c]), :].T
-                    for gl in range(2):
-                        for k in range(2):
-                            at = (2 * gl + k) * Q
-                            place(part, 2 * gh + gl, 16 + k, block[at : at + Q])
-
+                block = src[pl.ds(part * 8 + g * 2 + quad, NDEV, stride=PITCH[c]), :].T
+                for k in range(4):
+                    place(part, g, 8 * c + 4 * quad + k, block[k * Q : (k + 1) * Q])
+
+    def finish_last():
+        src = flat(v1, 1)
+        for part in range(2):
+            for gh in range(2):
+                block = src[pl.ds(16 + part * 2 + gh, NDEV, stride=PITCH[1]), :].T
+                for gl in range(2):
+                    for k in range(2):
+                        at = (2 * gl + k) * Q
+                        place(part, 2 * gh + gl, 16 + k, block[at : at + Q])
+
+    for copy in constants:
+        copy.wait()
     for c in range(2):
         arrived(lands[c], c, 0)
         transform(c)
         exchange(outs[c], backs[c], c, 1)
-    for c in range(2):
-        arrived(backs[c], c, 1)
-        finish(c)
+    arrived(v0, 0, 1)
+    finish(0, 0)
+    finish(0, 1)
+    write(0, 24).start()
+    arrived(v1, 1, 1)
+    finish(1, 0)
+    write(24, 24).start()
+    finish(1, 1)
+    finish_last()
+    write(48, 24).start()
     for c in range(2):
         sent(sends[c], c, 0)
         sent(outs[c], c, 1)
+    for n in range(3):
+        write(24 * n, 24).wait()
 
 
 def per_device(dynamical):
-    vmem = pl.BlockSpec(memory_space=pltpu.VMEM)
+    anywhere = pl.BlockSpec(memory_space=pl.ANY)
+    constants = tables()
     buffers = [pltpu.VMEM((NDEV, p, L), F32) for p in PITCH]
     return pl.pallas_call(
         kernel,
         out_shape=jax.ShapeDtypeStruct(dynamical.shape, F32),
-        in_specs=[vmem] * 4,
-        out_specs=vmem,
+        in_specs=[anywhere] * 4,
+        out_specs=anywhere,
         scratch_shapes=[
+            pltpu.VMEM(dynamical.shape, F32),
+            *[pltpu.VMEM(table.shape, table.dtype) for table in constants],
+            pltpu.VMEM(dynamical.shape, F32),
             pltpu.VMEM((2, Q * M, L), F32),
             *buffers, *buffers, *buffers, *buffers,
             pltpu.VMEM((4, 2 * L, 2 * L), BF16),
             pltpu.VMEM((4, 2 * L, 2 * L), BF16),
             pltpu.SemaphoreType.DMA((2, 2)),
             pltpu.SemaphoreType.DMA((2, 2)),
-            pltpu.SemaphoreType.REGULAR,
+            pltpu.SemaphoreType.DMA((LOCAL_X,)),
+            pltpu.SemaphoreType.DMA((3,)),
+            pltpu.SemaphoreType.DMA((3,)),
         ],
         compiler_params=pltpu.CompilerParams(
             collective_id=0, has_side_effects=True, vmem_limit_bytes=48 << 20
         ),
-    )(dynamical, *tables())
+    )(dynamical, *constants)
 
 
 def solution(mesh):

time: 92.1 us -> 78.5 us (0.85)
  Pallas kernels: 85.5 us -> 72.4 us
    pallas_call x1, Pallas kernels: 85.5 us -> 72.4 us  [per_device(): pl.pallas_call(kernel, out_shape=jax.ShapeDtypeStruct(dynamical.shape, F3...]
where the time goes in v2:
time: 78.5 us; the launch traced here: 78.3 us
  Pallas kernels  72.4 us (92%)
  local copies, waits for them, and re-layouts  5.88 us (7%)
    pallas_call x1, Pallas kernels, per_device(): pl.pallas_call(kernel, out_shape=jax.ShapeDtypeStruct(dynamical.shape, F3...  72.4 us
    unnamed x9, local copies, waits for them, and re-layouts  5.88 us

profile of v2, /device:TPU:1, one launch (start us, length us, event | category | flops | bytes accessed | tf_op | source)
XLA Modules:
  0.0 78.3 jit_solution(18034675601549860195)
XLA Ops:
  0.0 0.0 copy-start
  0.0 1.7 %copy-done = f32[2,4,8,9216]{3,2,1,0:T(8,128)S(1)} copy-done((f32[2,4,8,9216]{3,2,1,0:T(8,128)S(1)}, f32[2,4,8,9216]{3,2,1,0:T(8,128)}, u32[]{:S(2)}) %copy-start) | copy-done | bytes 2359320
  1.7 0.0 copy-start.1
  1.7 0.9 %copy-done.1 = bf16[512,256]{1,0:T(8,128)(2,1)S(1)} copy-done((bf16[512,256]{1,0:T(8,128)(2,1)S(1)}, bf16[512,256]{1,0:T(8,128)(2,1)}, u32[]{:S(2)}) %copy-start.1) | copy-done | bytes 262168
  2.6 0.0 copy-start.2
  2.6 0.9 %copy-done.2 = bf16[512,256]{1,0:T(8,128)(2,1)S(1)} copy-done((bf16[512,256]{1,0:T(8,128)(2,1)S(1)}, bf16[512,256]{1,0:T(8,128)(2,1)}, u32[]{:S(2)}) %copy-start.2) | copy-done | bytes 262168
  3.6 0.0 copy-start.3
  3.6 0.9 %copy-done.3 = f32[2,128,128]{2,1,0:T(8,128)S(1)} copy-done((f32[2,128,128]{2,1,0:T(8,128)S(1)}, f32[2,128,128]{2,1,0:T(8,128)}, u32[]{:S(2)}) %copy-start.3) | copy-done | bytes 131096
  4.5 72.4 %shard_map.46 = f32[2,4,8,9216]{3,2,1,0:T(8,128)S(1)} custom-call(f32[2,4,8,9216]{3,2,1,0:T(8,128)S(1)} %copy-done, bf16[512,256]{1,0:T(8,128)(2,1)S(1)} %copy-done.2, f32[2,128,128]{2,1,0:T(8,128)S(1)} %copy-done.3, bf16[512,256]{1,0:T(8,128)(2,1)S(1)} %copy-done.1), custom_call_target="tpu_custom_call" | custom-call | tf_op jit(solution)/shard_map/pallas_call | solution.py:365
  76.9 1.4 %copy.6 = f32[2,4,8,9216]{3,2,1,0:T(8,128)} copy(f32[2,4,8,9216]{3,2,1,0:T(8,128)S(1)} %shard_map.46) | data formatting | bytes 4718592
Async XLA Ops:
  0.0 1.7 %copy-start = (f32[2,4,8,9216]{3,2,1,0:T(8,128)S(1)}, f32[2,4,8,9216]{3,2,1,0:T(8,128)}, u32[]{:S(2)}) copy-start(f32[2,4,8,9216]{3,2,1,0:T(8,128)} %d_hbm.1) | copy-start | bytes 7077892
  1.7 0.9 %copy-start.1 = (bf16[512,256]{1,0:T(8,128)(2,1)S(1)}, bf16[512,256]{1,0:T(8,128)(2,1)}, u32[]{:S(2)}) copy-start(bf16[512,256]{1,0:T(8,128)(2,1)} %constant.8.clone.second_hbm) | copy-start | bytes 786436
  2.6 0.9 %copy-start.2 = (bf16[512,256]{1,0:T(8,128)(2,1)S(1)}, bf16[512,256]{1,0:T(8,128)(2,1)}, u32[]{:S(2)}) copy-start(bf16[512,256]{1,0:T(8,128)(2,1)} %constant.6.clone.first_hbm) | copy-start | bytes 786436
  3.6 0.9 %copy-start.3 = (f32[2,128,128]{2,1,0:T(8,128)S(1)}, f32[2,128,128]{2,1,0:T(8,128)}, u32[]{:S(2)}) copy-start(f32[2,128,128]{2,1,0:T(8,128)} %constant.7.clone.twiddle_hbm) | copy-start | bytes 393220

commit v3 on v2

--- a/solution.py
+++ b/solution.py
@@ -108,9 +108,9 @@
 
 
 def kernel(
-    d_hbm, first_hbm, twiddle_hbm, second_hbm, out_hbm,
-    d_ref, first_ref, twiddle_ref, second_ref, out_ref,
-    mat, s0, s1, r0, r1, t0, t1, v0, v1, up_h, up_l, ssem, rsem, dsem, csem, osem,
+    d_hbm, first_hbm, twiddle_hbm, second_hbm, out_ref,
+    d_ref, first_ref, twiddle_ref, second_ref,
+    mat, s0, s1, r0, r1, t0, t1, v0, v1, up_h, up_l, ssem, rsem, dsem, csem, both_sem,
 ):
     qx = lax.axis_index("qx")
     qy = lax.axis_index("qy")
@@ -131,14 +131,21 @@
 
     barrier = pltpu.get_barrier_semaphore()
 
-    def greet(o):
+    def hops(o):
+        return sum((0, 1, 2, 1)[o >> n & 3] for n in (1, 3, 5))
+
+    for o in [*sorted(range(2, NDEV, 2), key=hops, reverse=True), 1]:
         other = jnp.bitwise_xor(me, o)
         pl.semaphore_signal(
             barrier, inc=1, device_id=(other >> 3, other & 7), device_id_type=MESH
         )
 
-    for o in range(1, 4):
-        greet(o)
+    def all_entered():
+        pl.semaphore_wait(barrier, NDEV // 2)
+        pl.semaphore_signal(
+            both_sem, inc=1, device_id=(qx, jnp.bitwise_xor(qy, 1)), device_id_type=MESH
+        )
+        pl.semaphore_wait(both_sem, 1)
 
     def invert_some(x, carry):
         fetch(x).wait()
@@ -154,8 +161,6 @@
                     after = d_ref[part, x, :, (tile + 1) * L : (tile + 2) * L]
                     row = jnp.where(lane < L - off, row, pltpu.roll(after, L - off, 1))
                 mat[part, pl.ds(base + i, LOCAL_Y, stride=M), :] = row
-        for o in range(31):
-            greet(4 + x * 31 + o)
         rows = [pl.ds(pl.multiple_of(base + k * M, M), M) for k in range(LOCAL_Y)]
         results = invert([(mat[0, r, :], mat[1, r, :]) for r in rows])
         for r, result in zip(rows, results):
@@ -235,7 +240,7 @@
             for part in range(2):
                 pack(0, part, u, v, 0)
         if u == 2:
-            pl.semaphore_wait(barrier, NDEV - 1)
+            all_entered()
             exchange(s0, r0, 0, 0)
     exchange(s1, r1, 1, 0)
 
@@ -309,10 +314,6 @@
                             pl.ds((4 * jx + c0) * 8 * PITCH[c] + 16 + part * 2 + gh, 8, stride=PITCH[c]), :
                         ] = row
 
-    def write(tile, tiles):
-        part = pl.ds(tile * L, tiles * L)
-        return pltpu.make_async_copy(out_ref.at[:, :, :, part], out_hbm.at[:, :, :, part], osem.at[tile // 24])
-
     def place(part, g, row, block):
         tile = 12 * (row // 3) + 3 * g + row % 3
         out_ref[part, :, :, tile * L : (tile + 1) * L] = block.reshape(LOCAL_X, LOCAL_Y, L)
@@ -344,33 +345,30 @@
     arrived(v0, 0, 1)
     finish(0, 0)
     finish(0, 1)
-    write(0, 24).start()
     arrived(v1, 1, 1)
     finish(1, 0)
-    write(24, 24).start()
     finish(1, 1)
     finish_last()
-    write(48, 24).start()
     for c in range(2):
         sent(sends[c], c, 0)
         sent(outs[c], c, 1)
-    for n in range(3):
-        write(24 * n, 24).wait()
 
 
 def per_device(dynamical):
-    anywhere = pl.BlockSpec(memory_space=pl.ANY)
     constants = tables()
+    operands = [
+        pltpu.with_memory_space_constraint(operand, pltpu.HBM)
+        for operand in (dynamical, *map(jnp.asarray, constants))
+    ]
     buffers = [pltpu.VMEM((NDEV, p, L), F32) for p in PITCH]
     return pl.pallas_call(
         kernel,
-        out_shape=jax.ShapeDtypeStruct(dynamical.shape, F32),
-        in_specs=[anywhere] * 4,
-        out_specs=anywhere,
+        out_shape=pltpu.VMEM(dynamical.shape, F32),
+        in_specs=[pl.BlockSpec(memory_space=pltpu.HBM)] * 4,
+        out_specs=pl.BlockSpec(memory_space=pltpu.VMEM),
         scratch_shapes=[
             pltpu.VMEM(dynamical.shape, F32),
             *[pltpu.VMEM(table.shape, table.dtype) for table in constants],
-            pltpu.VMEM(dynamical.shape, F32),
             pltpu.VMEM((2, Q * M, L), F32),
             *buffers, *buffers, *buffers, *buffers,
             pltpu.VMEM((4, 2 * L, 2 * L), BF16),
@@ -379,12 +377,12 @@
             pltpu.SemaphoreType.DMA((2, 2)),
             pltpu.SemaphoreType.DMA((LOCAL_X,)),
             pltpu.SemaphoreType.DMA((3,)),
-            pltpu.SemaphoreType.DMA((3,)),
+            pltpu.SemaphoreType.REGULAR,
         ],
         compiler_params=pltpu.CompilerParams(
             collective_id=0, has_side_effects=True, vmem_limit_bytes=48 << 20
         ),
-    )(dynamical, *constants)
+    )(*operands)
 
 
 def solution(mesh):

time: 78.5 us -> 75.8 us (0.966)
  local copies, waits for them, and re-layouts: 5.88 us -> 1.41 us
  Pallas kernels: 72.4 us -> 74.3 us
    unnamed x9 -> x1, local copies, waits for them, and re-layouts: 5.88 us -> 1.41 us
    pallas_call x1, Pallas kernels: 72.4 us -> 74.3 us  [per_device(): pl.pallas_call(kernel, out_shape=pltpu.VMEM(dynamical.shape, F32), in_spe...]
where the time goes in v3:
time: 75.8 us; the launch traced here: 75.7 us
  Pallas kernels  74.3 us (98%)
  local copies, waits for them, and re-layouts  1.41 us (2%)
    pallas_call x1, Pallas kernels, per_device(): pl.pallas_call(kernel, out_shape=pltpu.VMEM(dynamical.shape, F32), in_spe...  74.3 us

profile of v3, /device:TPU:1, one launch (start us, length us, event | category | flops | bytes accessed | tf_op | source)
XLA Modules:
  0.0 75.7 jit_solution(8360071366754792877)
XLA Ops:
  0.0 74.3 %shard_map.46 = f32[2,4,8,9216]{3,2,1,0:T(8,128)S(1)} custom-call(f32[2,4,8,9216]{3,2,1,0:T(8,128)} %d_hbm.1, bf16[512,256]{1,0:T(8,128)(2,1)} %constant.6.clone.first_hbm, f32[2,128,128]{2,1,0:T(8,128)} %constant.7.clone.twiddle_hbm, bf16[512,256]{1,0:T(8,128)(2,1)} %constant.8.clone.second_hbm), custom_call_target="tpu_custom_call" | custom-call | tf_op jit(solution)/shard_map/pallas_call | solution.py:364
  74.3 1.4 %copy.6 = f32[2,4,8,9216]{3,2,1,0:T(8,128)} copy(f32[2,4,8,9216]{3,2,1,0:T(8,128)S(1)} %shard_map.46) | data formatting | bytes 4718592

commit v4 on v3

v4 whole, which is shorter than its diff:
```python
import functools

import jax
import jax.numpy as jnp
import ml_dtypes
import numpy as np
from jax import lax
from jax.experimental import pallas as pl
from jax.experimental.pallas import tpu as pltpu
from jax.sharding import PartitionSpec as P

M = 96
ETA = 0.25
NDEV = 128
SIZE_X, SIZE_Y = 16, 8
LOCAL_X, LOCAL_Y = 4, 8
Q = LOCAL_X * LOCAL_Y
L = 128
HALF = Q // 2
GROUPS = L // HALF
USED = (18, 8, 10, 16, 20)
PITCH = (24, 8, 16, 16, 24)
MESH = pl.DeviceIdType.MESH
F32 = jnp.float32
BF16 = jnp.bfloat16


def split_table(table):
    high = table.astype(ml_dtypes.bfloat16)
    low = (table - high.astype(np.float64)).astype(ml_dtypes.bfloat16)
    return high, low


def embed_table(angle):
    cosine, sine = np.cos(angle), np.sin(angle)
    return np.block([[cosine, -sine], [sine, cosine]])


def tables():
    ax, ay = np.divmod(np.arange(NDEV), SIZE_Y)
    turns = (ax[:, None] * ax[None, :] % 16) / 16 + (ay[:, None] * ay[None, :] % 8) / 8
    first = np.concatenate(split_table(embed_table(2 * np.pi * turns)), axis=0)
    lane = np.arange(L)
    group, bl, by = lane // HALF, lane % HALF // LOCAL_Y, lane % LOCAL_Y
    turns = np.stack(
        [
            (ax[:, None] * (2 * bh + bl)[None, :] + ay[:, None] * by[None, :]) / 64
            for bh in range(2)
        ]
    )
    twiddle = np.stack([np.cos(2 * np.pi * turns), np.sin(2 * np.pi * turns)], axis=1) / 64
    same = group[:, None] == group[None, :]
    second = []
    for j0 in range(2):
        turns = (2 * bl + j0)[:, None] * bl[None, :] / 4 + (by[:, None] * by[None, :] % 8) / 8
        cosine, sine = np.cos(2 * np.pi * turns) * same, np.sin(2 * np.pi * turns) * same
        table = split_table(np.block([[cosine, -sine], [sine, cosine]]))
        second.append(np.concatenate(table, axis=0))
    return first, twiddle.astype(np.float32), np.stack(second)


def split(value):
    high = value.astype(BF16)
    low = (value - high.astype(F32)).astype(BF16)
    return high, low


def dot(a, b, contract=0):
    return lax.dot_general(a, b, (((1,), (contract,)), ((), ())), preferred_element_type=F32)


def embed(part):
    zeros = jnp.zeros((L - M, 2 * L), part.dtype)
    real, imag = part[:, :L], part[:, L:]
    return jnp.concatenate(
        [part, zeros, jnp.concatenate([-imag, real], axis=1), zeros], axis=0
    )


def product(left, right):
    n = left[0].shape[0]
    both = dot(jnp.concatenate(left, axis=0), embed(right[0]))
    return both[:n] + both[n:] + dot(left[0], embed(right[1]))


def begin(real, imag):
    row = lax.broadcasted_iota(jnp.int32, (M, L), 0)
    col = lax.broadcasted_iota(jnp.int32, (M, L), 1)
    eye = row == col
    off = (col < M) & (row != col)
    diag = jnp.where(eye, real, 0.0)

    def start(d):
        denom = d * d + ETA * ETA
        return d / denom, -ETA / denom

    cr, ci = start(jnp.sum(diag, axis=0, keepdims=True))
    rr, ri = start(jnp.sum(diag, axis=1, keepdims=True))
    er = jnp.where(off, imag * ci - real * cr, 0.0)
    ei = jnp.where(off, -(real * ci + imag * cr), 0.0)
    pr = jnp.where(eye, 1.0, er)
    x1 = jnp.concatenate([rr * pr - ri * ei, rr * ei + ri * pr], axis=1)
    return x1, split(jnp.concatenate([er, ei], axis=1))


def stack(a, b):
    return tuple(jnp.concatenate(pair, axis=0) for pair in zip(a, b))


def invert(matrices):
    x1, e0 = zip(*[begin(*m) for m in matrices])
    e1 = [split(product(e, e)) for e in e0]
    both = [product(stack(split(x), e), e) for x, e in zip(x1, e1)]
    x2 = [x + b[:M] for x, b in zip(x1, both)]
    return [x + product(split(x), split(b[M:])) for x, b in zip(x2, both)]


def kernel(
    d_hbm, first_hbm, twiddle_hbm, second_hbm, out_ref,
    d_ref, first_ref, twiddle_ref, second_ref,
    mat, s0, s1, s2, t0, t1, r0, r1, r2, v0, v1, up_h, up_l, ssem, rsem, dsem, csem, both_sem,
):
    qx = lax.axis_index("qx")
    qy = lax.axis_index("qy")
    me = qx * SIZE_Y + qy

    def fetch(x):
        return pltpu.make_async_copy(d_hbm.at[:, x], d_ref.at[:, x], dsem.at[x])

    for x in range(LOCAL_X):
        fetch(x).start()
    constants = [
        pltpu.make_async_copy(first_hbm, first_ref, csem.at[0]),
        pltpu.make_async_copy(twiddle_hbm, twiddle_ref, csem.at[1]),
        pltpu.make_async_copy(second_hbm, second_ref, csem.at[2]),
    ]
    for copy in constants:
        copy.start()

    barrier = pltpu.get_barrier_semaphore()

    def hops(o):
        return sum((0, 1, 2, 1)[o >> n & 3] for n in (1, 3, 5))

    for o in [*sorted(range(2, NDEV, 2), key=hops, reverse=True), 1]:
        other = jnp.bitwise_xor(me, o)
        pl.semaphore_signal(
            barrier, inc=1, device_id=(other >> 3, other & 7), device_id_type=MESH
        )

    def all_entered():
        pl.semaphore_wait(barrier, NDEV // 2)
        pl.semaphore_signal(
            both_sem, inc=1, device_id=(qx, jnp.bitwise_xor(qy, 1)), device_id_type=MESH
        )
        pl.semaphore_wait(both_sem, 1)

    def invert_some(x, carry):
        fetch(x).wait()
        lane = lax.broadcasted_iota(jnp.int32, (LOCAL_Y, L), 1)
        base = x * (LOCAL_Y * M)
        for part in range(2):
            for i in range(M):
                tile, off = divmod(i * M, L)
                row = d_ref[part, x, :, tile * L : (tile + 1) * L]
                if off:
                    row = pltpu.roll(row, L - off, 1)
                if off + M > L:
                    after = d_ref[part, x, :, (tile + 1) * L : (tile + 2) * L]
                    row = jnp.where(lane < L - off, row, pltpu.roll(after, L - off, 1))
                mat[part, pl.ds(base + i, LOCAL_Y, stride=M), :] = row
        rows = [pl.ds(pl.multiple_of(base + k * M, M), M) for k in range(LOCAL_Y)]
        results = invert([(mat[0, r, :], mat[1, r, :]) for r in rows])
        for r, result in zip(rows, results):
            mat[0, r, :] = result[:, :L]
            mat[1, r, :] = result[:, L:]
        return carry

    sources = (s0, s1, s2, t0, t1)
    places = (r0, r1, r2, v0, v1)

    def exchange(c):
        src, dst = sources[c], places[c]
        used = pl.ds(0, USED[c])
        own = pltpu.make_async_copy(src.at[me, used], dst.at[me, used], rsem.at[c])
        own.start()

        def send(o, carry):
            z, x, y, h = qx >> 2, (qx & 3) + (o & 3), (qy >> 1) + (o >> 2), qy & 1
            for n in range(8):
                k, core = n & 3, n >> 2
                tx = (((z + k) & 3) << 2) | ((x + k) & 3)
                ty = (((y + k) & 3) << 1) | (h ^ core)
                target = (tx << 3) | ty

                def start():
                    pltpu.make_async_remote_copy(
                        src_ref=src.at[target, used],
                        dst_ref=dst.at[me, used],
                        send_sem=ssem.at[c],
                        recv_sem=rsem.at[c],
                        device_id=(tx, ty),
                        device_id_type=MESH,
                    ).start()

                if n == 0:
                    pl.when(target != me)(start)
                else:
                    start()
            return carry

        lax.fori_loop(0, NDEV // 8, send, 0)

    def arrived(c):
        whole = places[c].at[:, pl.ds(0, USED[c])]
        pltpu.make_async_copy(whole, whole, rsem.at[c]).wait()

    def sent(c):
        whole = sources[c].at[pl.ds(0, NDEV - 1), pl.ds(0, USED[c])]
        pltpu.make_async_copy(whole, whole, ssem.at[c]).wait()

    def flat(ref, c):
        return ref.reshape(NDEV * PITCH[c], L)

    def pack(half, u):
        for v in range(4):
            for part in range(2):
                first = half * HALF * M + 4 * GROUPS * u + v
                block = jnp.concatenate(
                    [mat[part, pl.ds(first + 4 * g, HALF, stride=M), :] for g in range(GROUPS)], axis=0
                ).T
                for w in range(3):
                    lo, hi = max(0, w * L - v * M), min(M, (w + 1) * L - v * M)
                    if lo >= hi:
                        continue
                    row = 3 * u + w
                    if half == 0:
                        c, row = 0, part * 9 + row
                    elif row < 4:
                        c, row = 1, part * 4 + row
                    else:
                        c, row = 2, part * 5 + row - 4
                    at = (v * M + lo - w * L) * PITCH[c] + row
                    flat(sources[c], c)[pl.ds(at, hi - lo, stride=PITCH[c]), :] = block[lo:hi]

    def stage_one(row):
        c, first, count = (1, row, 4) if row < 4 else (2, row - 4, 5)
        cols = []
        for src, at, step in ((0, row, 9), (c, first, count)):
            ref = flat(places[src], src)
            cols.append(
                jnp.concatenate(
                    [ref[pl.ds(part * step + at, NDEV, stride=PITCH[src]), :] for part in range(2)], axis=0
                )
            )
        high, low = split(jnp.concatenate(cols, axis=1))
        table = first_ref[...]
        both = dot(table, high)
        total = both[: 2 * L] + both[2 * L :] + dot(table[: 2 * L], low)
        turned = []
        for bh in range(2):
            real, imag = total[:L, bh * L : (bh + 1) * L], total[L:, bh * L : (bh + 1) * L]
            tr, ti = twiddle_ref[bh, 0], twiddle_ref[bh, 1]
            turned.append(jnp.concatenate([real * tr - imag * ti, real * ti + imag * tr], axis=1))
        return turned[0] + turned[1], turned[0] - turned[1]

    def keep(row, at, pitch):
        for j0, value in enumerate(stage_one(row)):
            high, low = split(value)
            for c0 in range(4):
                rows = slice(c0 * pitch + at, c0 * pitch + at + Q)
                up_h[j0, rows, :] = high[c0 * Q : (c0 + 1) * Q]
                up_l[j0, rows, :] = low[c0 * Q : (c0 + 1) * Q]

    def stage_two(j0, rows):
        table = second_ref[j0]
        both = dot(table, up_h[j0, rows, :], 1)
        return both[: 2 * L] + both[2 * L :] + dot(table[: 2 * L], up_l[j0, rows, :], 1)

    def put(c, jx, c0, row, value):
        at = (4 * jx + c0) * LOCAL_Y * PITCH[c] + row
        flat(sources[c], c)[pl.ds(at, LOCAL_Y, stride=PITCH[c]), :] = value

    def transform(n):
        c = 3 + n
        for k in range(4):
            keep(4 * n + k, k * Q, L)
        for j0 in range(2):
            for pair in range(2):
                result = stage_two(j0, slice(pair * 2 * L, (pair + 1) * 2 * L))
                for part in range(2):
                    for g in range(GROUPS):
                        for j1 in range(2):
                            r = part * L + g * HALF + j1 * LOCAL_Y
                            for k in range(2):
                                put(
                                    c, 2 * j1 + j0, 2 * pair + k, part * GROUPS + g,
                                    result[r : r + LOCAL_Y, k * L : (k + 1) * L],
                                )
        if n == 0:
            return
        keep(8, 0, Q)
        lane = lax.broadcasted_iota(jnp.int32, (LOCAL_Y, L), 1)
        for j0 in range(2):
            result = stage_two(j0, slice(0, L))
            for part in range(2):
                for gh in range(2):
                    for j1 in range(2):
                        r = part * L + gh * 4 * HALF + j1 * LOCAL_Y
                        parts = [result[r + gl * HALF : r + gl * HALF + LOCAL_Y] for gl in range(4)]
                        for c0 in range(4):
                            row = parts[c0]
                            for gl in range(4):
                                if gl != c0:
                                    moved = pltpu.roll(parts[gl], (gl - c0) % 4 * Q, 1)
                                    row = jnp.where(lane // Q == gl, moved, row)
                            put(c, 2 * j1 + j0, c0, 2 * GROUPS + part * 2 + gh, row)

    def place(part, g, row, block):
        tile = 24 * (row // 3) + 3 * g + row % 3
        out_ref[part, :, :, tile * L : (tile + 1) * L] = block.reshape(LOCAL_X, LOCAL_Y, L)

    def finish(n):
        c = 3 + n
        src = flat(places[c], c)
        for part in range(2):
            for g in range(GROUPS):
                block = src[pl.ds(part * GROUPS + g, NDEV, stride=PITCH[c]), :].T
                for k in range(4):
                    place(part, g, 4 * n + k, block[k * Q : (k + 1) * Q])
            if n == 1:
                for gh in range(2):
                    block = src[pl.ds(2 * GROUPS + part * 2 + gh, NDEV, stride=PITCH[c]), :].T
                    for gl in range(4):
                        place(part, 4 * gh + gl, 8, block[gl * Q : (gl + 1) * Q])

    lax.fori_loop(0, LOCAL_X // 2, invert_some, 0)
    for u in range(3):
        pack(0, u)
    all_entered()
    exchange(0)
    lax.fori_loop(LOCAL_X // 2, LOCAL_X, invert_some, 0)
    pack(1, 0)
    pack(1, 1)
    exchange(1)
    pack(1, 2)
    exchange(2)
    for copy in constants:
        copy.wait()
    arrived(0)
    for n in range(2):
        arrived(1 + n)
        transform(n)
        exchange(3 + n)
    for n in range(2):
        arrived(3 + n)
        finish(n)
    for c in range(5):
        sent(c)


def per_device(dynamical):
    constants = tables()
    operands = [
        pltpu.with_memory_space_constraint(operand, pltpu.HBM)
        for operand in (dynamical, *map(jnp.asarray, constants))
    ]
    buffers = [pltpu.VMEM((NDEV, p, L), F32) for p in PITCH]
    return pl.pallas_call(
        kernel,
        out_shape=pltpu.VMEM(dynamical.shape, F32),
        in_specs=[pl.BlockSpec(memory_space=pltpu.HBM)] * 4,
        out_specs=pl.BlockSpec(memory_space=pltpu.VMEM),
        scratch_shapes=[
            pltpu.VMEM(dynamical.shape, F32),
            *[pltpu.VMEM(table.shape, table.dtype) for table in constants],
            pltpu.VMEM((2, Q * M, L), F32),
            *buffers, *buffers,
            pltpu.VMEM((2, 4 * L, 2 * L), BF16),
            pltpu.VMEM((2, 4 * L, 2 * L), BF16),
            pltpu.SemaphoreType.DMA((5,)),
            pltpu.SemaphoreType.DMA((5,)),
            pltpu.SemaphoreType.DMA((LOCAL_X,)),
            pltpu.SemaphoreType.DMA((3,)),
            pltpu.SemaphoreType.REGULAR,
        ],
        compiler_params=pltpu.CompilerParams(
            collective_id=0, has_side_effects=True, vmem_limit_bytes=48 << 20
        ),
    )(*operands)


def solution(mesh):
    return jax.shard_map(
        per_device,
        mesh=mesh,
        in_specs=(P(None, "qx", "qy", None),),
        out_specs=P(None, "qx", "qy", None),
        check_vma=False,
    )
```

time: 75.8 us -> 69.6 us (0.918)
  Pallas kernels: 74.3 us -> 68 us
    pallas_call x1, Pallas kernels: 74.3 us -> 68 us  [per_device(): pl.pallas_call(kernel, out_shape=pltpu.VMEM(dynamical.shape, F32), in_spe...]
where the time goes in v4:
time: 69.6 us; the launch traced here: 69.5 us
  Pallas kernels  68 us (98%)
  local copies, waits for them, and re-layouts  1.41 us (2%)
    pallas_call x1, Pallas kernels, per_device(): pl.pallas_call(kernel, out_shape=pltpu.VMEM(dynamical.shape, F32), in_spe...  68 us
    unnamed x1, local copies, waits for them, and re-layouts  1.41 us

profile of v4, /device:TPU:1, one launch (start us, length us, event | category | flops | bytes accessed | tf_op | source)
XLA Modules:
  0.0 69.5 jit_solution(17119966589558989100)
XLA Ops:
  0.0 68.0 %shard_map.46 = f32[2,4,8,9216]{3,2,1,0:T(8,128)S(1)} custom-call(f32[2,4,8,9216]{3,2,1,0:T(8,128)} %d_hbm.1, bf16[512,256]{1,0:T(8,128)(2,1)} %constant.6.clone.first_hbm, f32[2,2,128,128]{3,2,1,0:T(8,128)} %constant.7.clone.twiddle_hbm, bf16[2,512,256]{2,1,0:T(8,128)(2,1)} %constant.8.clone.second_hbm), custom_call_target="tpu_custom_call" | custom-call | tf_op jit(solution)/shard_map/pallas_call | solution.py:369
  68.1 1.4 %copy.6 = f32[2,4,8,9216]{3,2,1,0:T(8,128)} copy(f32[2,4,8,9216]{3,2,1,0:T(8,128)S(1)} %shard_map.46) | data formatting | bytes 4718592

commit v5 on v4

--- a/solution.py
+++ b/solution.py
@@ -212,7 +212,7 @@
         lax.fori_loop(0, NDEV // 8, send, 0)
 
     def arrived(c):
-        whole = places[c].at[:, pl.ds(0, USED[c])]
+        whole = places[c].at[pl.ds(0, NDEV), pl.ds(0, USED[c])]
         pltpu.make_async_copy(whole, whole, rsem.at[c]).wait()
 
     def sent(c):
@@ -220,7 +220,7 @@
         pltpu.make_async_copy(whole, whole, ssem.at[c]).wait()
 
     def flat(ref, c):
-        return ref.reshape(NDEV * PITCH[c], L)
+        return ref.reshape((NDEV + 1) * PITCH[c], L)
 
     def pack(half, u):
         for v in range(4):
@@ -365,7 +365,7 @@
         pltpu.with_memory_space_constraint(operand, pltpu.HBM)
         for operand in (dynamical, *map(jnp.asarray, constants))
     ]
-    buffers = [pltpu.VMEM((NDEV, p, L), F32) for p in PITCH]
+    buffers = [pltpu.VMEM((NDEV + 1, p, L), F32) for p in PITCH]
     return pl.pallas_call(
         kernel,
         out_shape=pltpu.VMEM(dynamical.shape, F32),
@@ -374,7 +374,7 @@
         scratch_shapes=[
             pltpu.VMEM(dynamical.shape, F32),
             *[pltpu.VMEM(table.shape, table.dtype) for table in constants],
-            pltpu.VMEM((2, Q * M, L), F32),
+            pltpu.VMEM((2, (Q + 1) * M, L), F32),
             *buffers, *buffers,
             pltpu.VMEM((2, 4 * L, 2 * L), BF16),
             pltpu.VMEM((2, 4 * L, 2 * L), BF16),

time: 69.6 us -> 69.5 us (level)
  no operation moved by 1% of the time
where the time goes in v5:
time: 69.5 us; the launch traced here: 69.4 us
  Pallas kernels  68 us (98%)
  local copies, waits for them, and re-layouts  1.41 us (2%)
    pallas_call x1, Pallas kernels, per_device(): pl.pallas_call(kernel, out_shape=pltpu.VMEM(dynamical.shape, F32), in_spe...  68 us
    unnamed x1, local copies, waits for them, and re-layouts  1.41 us

profile of v5, /device:TPU:1, one launch (start us, length us, event | category | flops | bytes accessed | tf_op | source)
XLA Modules:
  0.0 69.4 jit_solution(12500809276682041029)
XLA Ops:
  0.0 68.0 %shard_map.46 = f32[2,4,8,9216]{3,2,1,0:T(8,128)S(1)} custom-call(f32[2,4,8,9216]{3,2,1,0:T(8,128)} %d_hbm.1, bf16[512,256]{1,0:T(8,128)(2,1)} %constant.6.clone.first_hbm, f32[2,2,128,128]{3,2,1,0:T(8,128)} %constant.7.clone.twiddle_hbm, bf16[2,512,256]{2,1,0:T(8,128)(2,1)} %constant.8.clone.second_hbm), custom_call_target="tpu_custom_call" | custom-call | tf_op jit(solution)/shard_map/pallas_call | solution.py:369
  68.0 1.4 %copy.6 = f32[2,4,8,9216]{3,2,1,0:T(8,128)} copy(f32[2,4,8,9216]{3,2,1,0:T(8,128)S(1)} %shard_map.46) | data formatting | bytes 4718592

commit v6 on v5

--- a/solution.py
+++ b/solution.py
@@ -155,7 +155,7 @@
         )
         pl.semaphore_wait(both_sem, 1)
 
-    def invert_some(x, carry):
+    def unflatten(x):
         fetch(x).wait()
         lane = lax.broadcasted_iota(jnp.int32, (LOCAL_Y, L), 1)
         base = x * (LOCAL_Y * M)
@@ -169,12 +169,14 @@
                     after = d_ref[part, x, :, (tile + 1) * L : (tile + 2) * L]
                     row = jnp.where(lane < L - off, row, pltpu.roll(after, L - off, 1))
                 mat[part, pl.ds(base + i, LOCAL_Y, stride=M), :] = row
+
+    def invert_at(x):
+        base = x * (LOCAL_Y * M)
         rows = [pl.ds(pl.multiple_of(base + k * M, M), M) for k in range(LOCAL_Y)]
         results = invert([(mat[0, r, :], mat[1, r, :]) for r in rows])
         for r, result in zip(rows, results):
             mat[0, r, :] = result[:, :L]
             mat[1, r, :] = result[:, L:]
-        return carry
 
     sources = (s0, s1, s2, t0, t1)
     places = (r0, r1, r2, v0, v1)
@@ -334,12 +336,20 @@
                     for gl in range(4):
                         place(part, 4 * gh + gl, 8, block[gl * Q : (gl + 1) * Q])
 
-    lax.fori_loop(0, LOCAL_X // 2, invert_some, 0)
+    unflatten(0)
+    unflatten(1)
+    invert_at(0)
+    invert_at(1)
     for u in range(3):
         pack(0, u)
     all_entered()
     exchange(0)
-    lax.fori_loop(LOCAL_X // 2, LOCAL_X, invert_some, 0)
+    def rest(x, carry):
+        unflatten(x)
+        invert_at(x)
+        return carry
+
+    lax.fori_loop(LOCAL_X // 2, LOCAL_X, rest, 0)
     pack(1, 0)
     pack(1, 1)
     exchange(1)

time: 69.5 us -> 69.2 us (level)
  no operation moved by 1% of the time
where the time goes in v6:
time: 69.2 us; the launch traced here: 69.1 us
  Pallas kernels  67.7 us (98%)
  local copies, waits for them, and re-layouts  1.41 us (2%)
    pallas_call x1, Pallas kernels, per_device(): pl.pallas_call(kernel, out_shape=pltpu.VMEM(dynamical.shape, F32), in_spe...  67.7 us
    unnamed x1, local copies, waits for them, and re-layouts  1.41 us

profile of v6, /device:TPU:1, one launch (start us, length us, event | category | flops | bytes accessed | tf_op | source)
XLA Modules:
  0.0 69.1 jit_solution(10450623169776563747)
XLA Ops:
  0.0 67.7 %shard_map.46 = f32[2,4,8,9216]{3,2,1,0:T(8,128)S(1)} custom-call(f32[2,4,8,9216]{3,2,1,0:T(8,128)} %d_hbm.1, bf16[512,256]{1,0:T(8,128)(2,1)} %constant.6.clone.first_hbm, f32[2,2,128,128]{3,2,1,0:T(8,128)} %constant.7.clone.twiddle_hbm, bf16[2,512,256]{2,1,0:T(8,128)(2,1)} %constant.8.clone.second_hbm), custom_call_target="tpu_custom_call" | custom-call | tf_op jit(solution)/shard_map/pallas_call | solution.py:379
  67.7 1.4 %copy.6 = f32[2,4,8,9216]{3,2,1,0:T(8,128)} copy(f32[2,4,8,9216]{3,2,1,0:T(8,128)S(1)} %shard_map.46) | data formatting | bytes 4718592
